TPU v7x, 32 devices: a whole 2x2x4 slice. The times are simulated.
32 devices in a mesh: groups: 2 (over y), chan: 4 (over z), win: 2 (over x), lag: 2 (over core).
Axes of the slice: x: 2, y: 2, z: 4, core: 2. Of those that a mesh axis runs over, the one named last changes fastest.
Arguments:
- spectra: bfloat16 [32, 2, 256, 1024], P('win', None, ('groups', 'chan'), 'lag'), parts along dimension 2, may hold values from -6 to 6
- dead_mask: int32 [256], P(('groups', 'chan')), parts along dimension 0, may hold values 0 or 1
- partners: int32 [4, 4], replicated, may hold values from -1 to 3, as said below
Outputs:
- correlations: float32 [256, 4, 32, 512], P(('groups', 'chan'), None, 'win', 'lag'), parts along dimension 0
There are 2 independent parts, one for each index of `groups`. A program takes and returns all parts, laid end to end along the dimension named above; an argument that names none is the same for every part. Nothing has to cross between parts.
Inputs may be any that keep to these rules, and one draw needn't show every extreme that they name: `partners`: row p lists the blocks p, p + 1, ... up to p + r - 1, where the reach r of 1 to 4 is drawn for each row and is 4 in row 0; blocks past the last and slots past the reach hold -1.
All inputs are finite; a program needn't handle non-finite values. No bound on the sum of `dead_mask` on one device may be relied on, other than what follows from the above.
Results may differ from a plain program's by a relative error of at most 0.0024.
Values may be sent and summed in bfloat16 or wider, within the bound.
A program may use at most 192 MiB of HBM per device.

v0:
```python
import math

import jax
import jax.numpy as jnp
from jax import lax
from jax.sharding import PartitionSpec as P

LAGS = 512
NSAMP = 15000
FLOW = 60


water_level = 0.5


def shifted(block, axis, distance):
    devices = range(lax.axis_size(axis))
    route = [(i - distance, i) for i in devices if i - distance in devices]
    return lax.ppermute(block, axis, route)


def whiten(spectra, dead_mask):
    values = spectra.astype(jnp.float32)
    amplitude = jnp.sqrt(values[:, 0] * values[:, 0] + values[:, 1] * values[:, 1])
    factor = dead_mask.astype(jnp.float32)[None, :, None] / jnp.maximum(amplitude, water_level)
    return (values * factor[:, None]).astype(jnp.bfloat16)


def phase_table(first_bin, bin_count):
    bins = FLOW + first_bin + jnp.arange(bin_count, dtype=jnp.int32)
    offsets = jnp.arange(LAGS, dtype=jnp.int32) - LAGS // 2
    turns = jnp.mod(bins[:, None] * offsets[None, :], NSAMP)
    angle = turns.astype(jnp.float32) * (2.0 * math.pi / NSAMP)
    return jnp.concatenate([jnp.cos(angle), -jnp.sin(angle)], axis=0)


def cross_spectra(own_block, partner):
    pattern = "waf,wkjf->akjf"
    real_in = partner[:, :, 0]
    imag_in = partner[:, :, 1]

    def product(left, right):
        return jnp.einsum(pattern, left, right, preferred_element_type=jnp.float32)

    real_part = product(own_block[:, 0], real_in) + product(own_block[:, 1], imag_in)
    imag_part = product(own_block[:, 1], real_in) - product(own_block[:, 0], imag_in)
    return jnp.stack([real_part, imag_part], axis=3)


def transform(stacked, table):
    shape = stacked.shape
    flat = stacked.reshape(shape[0] * shape[1] * shape[2], shape[3] * shape[4])
    result = jnp.dot(
        flat, table, precision=lax.Precision.HIGHEST, preferred_element_type=jnp.float32
    )
    return result.reshape(shape[0], shape[1], shape[2], table.shape[1])


def body(spectra, dead_mask, partners):
    whitened = whiten(spectra, dead_mask)
    bin_count = whitened.shape[3]
    wanted_blocks = lax.dynamic_index_in_dim(partners, lax.axis_index("chan"), 0, keepdims=False)
    slot_count = wanted_blocks.shape[0]
    pieces = [whitened]
    for offset in range(1, slot_count):
        pieces.append(shifted(whitened, "chan", -offset))
    usable = (wanted_blocks >= 0).astype(jnp.bfloat16)
    table = phase_table(lax.axis_index("lag") * bin_count, bin_count)
    win_count = lax.axis_size("win")
    partner_local = jnp.stack(pieces, axis=1) * usable[None, :, None, None, None]
    own_all = lax.all_gather(whitened, "win", axis=0, tiled=True)
    partner_all = lax.all_to_all(partner_local, "win", split_axis=3, concat_axis=0, tiled=True)
    partial_value = transform(cross_spectra(own_all, partner_all), table)
    summed = lax.psum_scatter(partial_value, "lag", scatter_dimension=3, tiled=True)
    scale = (whitened.shape[0] * win_count * bin_count * lax.axis_size("lag")) ** (-0.5)
    return summed * scale


def solution(mesh):
    placed = (P("win", None, ("groups", "chan"), "lag"), P(("groups", "chan")), P())
    return jax.shard_map(
        body,
        mesh=mesh,
        in_specs=placed,
        out_specs=P(("groups", "chan"), None, "win", "lag"),
        check_vma=False,
    )
```

profile of v0, /device:TPU:0, one launch (start us, length us, event | category | flops | bytes accessed | tf_op | source)
XLA Modules:
  0.0 338.4 jit_solution(2257904631185280313)
XLA Ops:
  6.5 0.0 copy-start.2
  6.5 0.0 all-gather.2.cloned.1.call-start
  6.5 1.6 convert_element_type.22
  8.1 0.7 convert_element_type.23
  8.8 0.5 fusion.19
  9.3 0.0 copy-done.2
  9.3 0.3 multiply_convert_fusion
  9.6 0.0 copy-start.4
  9.6 1.3 collective-permute-start
  10.9 1.3 collective-permute-start.1
  12.2 1.3 collective-permute-start.2
  13.5 0.0 copy-done.4
  13.5 0.0 all-gather.2.cloned.1.call-update
  13.5 0.7 fusion.24
  14.2 0.3 fusion.29
  14.5 23.3 %collective-permute-done = bf16[16,2,32,512]{3,2,1,0:T(8,128)(2,1)} collective-permute-done((bf16[16,2,32,512]{3,2,1,0:T(8,128)(2,1)S(1)}, bf16[16,2,32,512]{3,2,1,0:T(8,128)(2,1)}, u32[]{:S(2)}, u32[]{:S(2)}) %collective-permute-start) | collective-permute-done | bytes 1048608 | tf_op jit(solution)/shard_map/ppermute | solution.py:19
  37.8 68.6 %collective-permute-done.1 = bf16[16,2,32,512]{3,2,1,0:T(8,128)(2,1)} collective-permute-done((bf16[16,2,32,512]{3,2,1,0:T(8,128)(2,1)S(1)}, bf16[16,2,32,512]{3,2,1,0:T(8,128)(2,1)}, u32[]{:S(2)}, u32[]{:S(2)}) %collective-permute-start.1) | collective-permute-done | bytes 1048608 | tf_op jit(solution)/shard_map/ppermute | solution.py:19
  106.4 0.0 collective-permute-done.2
  106.4 2.2 maximum_multiply_fusion
  108.5 4.4 %copy.52 = bf16[16,4,2,32,512]{4,0,2,1,3:T(8,128)(2,1)} copy(bf16[16,4,2,32,512]{4,3,2,1,0:T(8,128)(2,1)S(1)} %maximum_multiply_fusion) | data formatting | bytes 8388608 | tf_op jit(solution)/shard_map/mul | solution.py:70
  112.9 5.6 %all-to-all-start = ((bf16[16,4,2,32,512]{4,0,2,1,3:T(8,128)(2,1)}), bf16[16,4,2,32,512]{4,0,2,1,3:T(8,128)(2,1)}, u32[]{:S(2)}, u32[]{:S(2)}) async-start(bf16[16,4,2,32,512]{4,0,2,1,3:T(8,128)(2,1)} %copy.52), calls=%async_computation | async-start | bytes 8388608 | tf_op jit(solution)/shard_map/all_to_all | solution.py:72
  118.5 0.2 reduce-scatter.2.cloned.1.call-start
  118.8 5.3 %fusion.22 = (f32[512,512]{1,0:T(8,128)S(1)}, f32[512,512]{1,0:T(8,128)}) fusion(s32[512]{0:T(512)S(1)} %get-tuple-element.11, s32[512]{0:T(512)S(1)} %get-tuple-element.12), kind=kLoop, calls=%fused_computation.34 | loop fusion | flops 2621440 | bytes 2101248 | tf_op jit(solution)/shard_map/cos | solution.py:34
  124.1 0.0 all-gather.2.cloned.1.call-done
  124.1 1.7 fusion.27
  125.8 6.5 %copy.65 = bf16[32,1,32,512]{2,0,3,1:T(8,128)(2,1)} copy(bf16[32,1,32,512]{3,2,1,0:T(8,128)(2,1)S(1)} %get-tuple-element.7) | data formatting | bytes 2097152
  132.3 6.5 %copy.67 = bf16[32,1,32,512]{2,0,3,1:T(8,128)(2,1)} copy(bf16[32,1,32,512]{3,2,1,0:T(8,128)(2,1)S(1)} %get-tuple-element.8) | data formatting | bytes 2097152
  138.8 26.5 %all-to-all-done = bf16[16,4,2,32,512]{4,0,2,1,3:T(8,128)(2,1)} async-done(((bf16[16,4,2,32,512]{4,0,2,1,3:T(8,128)(2,1)}), bf16[16,4,2,32,512]{4,0,2,1,3:T(8,128)(2,1)}, u32[]{:S(2)}, u32[]{:S(2)}) %all-to-all-start) | async-done | bytes 4194336 | tf_op jit(solution)/shard_map/all_to_all | solution.py:72
  165.3 4.5 %copy.54 = bf16[2,16,4,2,16,512]{5,4,3,2,1,0:T(8,128)(2,1)S(1)} copy(bf16[2,16,4,2,16,512]{5,1,3,2,4,0:T(8,128)(2,1)} %bitcast.8) | data formatting | bytes 8388608 | tf_op jit(solution)/shard_map/all_to_all | solution.py:72
  169.8 1.8 fusion.26
  171.6 15.3 %copy.64 = bf16[32,4,1,16,512]{0,3,1,4,2:T(8,128)(2,1)} copy(bf16[32,4,1,16,512]{4,3,2,1,0:T(8,128)(2,1)} %get-tuple-element.6) | data formatting | bytes 4194304
  186.9 12.8 %copy.66 = bf16[32,4,1,16,512]{0,3,1,4,2:T(8,128)(2,1)} copy(bf16[32,4,1,16,512]{4,3,2,1,0:T(8,128)(2,1)S(1)} %get-tuple-element.5) | data formatting | bytes 4194304
  199.7 0.0 copy-start
  199.7 0.0 copy-start.1
  199.7 12.8 %fusion.4 = f32[512,4,16,32]{3,2,1,0:T(8,128)} fusion(bf16[32,4,1,16,512]{0,3,1,4,2:T(8,128)(2,1)} %copy.64, bf16[32,1,32,512]{2,0,3,1:T(8,128)(2,1)} %copy.65), kind=kOutput, calls=%fused_computation.7 | convolution fusion | flops 67108864 | bytes 7340032 | tf_op jit(solution)/shard_map/waf,wkjf->akjf/dot_general | solution.py:43
  212.5 0.0 copy-done
  212.5 0.0 copy-done.1
  212.5 7.0 %fusion.2 = f32[512,4,16,32]{3,2,1,0:T(8,128)} fusion(bf16[32,4,1,16,512]{0,3,1,4,2:T(8,128)(2,1)S(1)} %copy-done, bf16[32,1,32,512]{2,0,3,1:T(8,128)(2,1)S(1)} %copy-done.1), kind=kOutput, calls=%fused_computation.5 | convolution fusion | flops 67108864 | bytes 7340032 | tf_op jit(solution)/shard_map/waf,wkjf->akjf/dot_general | solution.py:43
  219.4 17.5 %add_bitcast_fusion = f32[32,4,16,1,512]{0,2,1,4,3:T(8,128)} fusion(f32[512,4,16,32]{3,2,1,0:T(8,128)} %fusion.4, bf16[32,4,1,16,512]{0,3,1,4,2:T(8,128)(2,1)} %copy.66, bf16[32,1,32,512]{2,0,3,1:T(8,128)(2,1)} %copy.67), kind=kOutput, calls=%fused_computation.2 | convolution fusion | flops 68157440 | bytes 11534336 | tf_op jit(solution)/shard_map/waf,wkjf->akjf/dot_general | solution.py:43
  236.9 17.5 %subtract_bitcast_fusion = f32[32,4,16,1,512]{0,2,1,4,3:T(8,128)} fusion(f32[512,4,16,32]{3,2,1,0:T(8,128)} %fusion.2, bf16[32,4,1,16,512]{0,3,1,4,2:T(8,128)(2,1)} %copy.66, bf16[32,1,32,512]{2,0,3,1:T(8,128)(2,1)} %copy.65), kind=kOutput, calls=%fused_computation.1 | convolution fusion | flops 68157440 | bytes 11534336 | tf_op jit(solution)/shard_map/waf,wkjf->akjf/dot_general | solution.py:43
  254.4 24.5 %pad_maximum_fusion = f32[32,4,16,2,512]{0,2,1,4,3:T(8,128)} fusion(f32[32,4,16,1,512]{0,2,1,4,3:T(8,128)} %subtract_bitcast_fusion, f32[32,4,16,1,512]{0,2,1,4,3:T(8,128)} %add_bitcast_fusion), kind=kLoop, calls=%fused_computation | loop fusion | flops 2097152 | bytes 16777216 | tf_op jit(solution)/shard_map/stack | solution.py:47
  278.9 0.0 copy-start.3
  278.9 22.9 %copy.59 = f32[32,4,16,1024]{3,2,1,0:T(8,128)} copy(f32[32,4,16,1024]{0,2,1,3:T(8,128)} %bitcast.54) | data formatting | bytes 16777216 | tf_op jit(solution)/shard_map/dot_general | solution.py:53
  301.8 0.0 copy-done.3
  301.8 16.9 %fusion.10 = f32[32,4,16,512]{3,2,1,0:T(8,128)} fusion(f32[32,4,16,1024]{3,2,1,0:T(8,128)} %copy.59, f32[512,512]{1,0:T(8,128)S(1)} %copy-done.3, f32[512,512]{1,0:T(8,128)S(1)} %get-tuple-element.9), kind=kOutput, calls=%fused_computation.15 | convolution fusion | flops 12885426176 | bytes 14680064 | tf_op jit(solution)/shard_map/dot_general | solution.py:53
  318.7 0.0 reduce-scatter.2.cloned.1.call-update
  318.8 9.5 %reduce-scatter.2.cloned.1.call-done = f32[32,4,16,256]{3,2,1,0:T(8,128)} async-done(((f32[32,4,16,512]{3,2,1,0:T(8,128)}), f32[32,4,16,256]{3,2,1,0:T(8,128)}) %reduce-scatter.2.cloned.1.call-update) | async-done | bytes 2097168 | tf_op jit(solution)/shard_map/reduce_scatter | solution.py:74
  328.3 3.3 broadcast_multiply_fusion
  (1 shorter events, 0.0 us)
Async XLA Ops:
  6.5 2.7 copy-start.2
  6.5 117.6 %all-gather.2.cloned.1.call-start = ((), (), s32[]{:S(2)}) async-start(), calls=%async_computation.2 | async-start | bytes 3145728 | tf_op jit(solution)/shard_map/all_gather | solution.py:71
  9.6 3.9 %copy-start.4 = (bf16[16,2,32,512]{3,2,1,0:T(8,128)(2,1)}, bf16[16,2,32,512]{3,2,1,0:T(8,128)(2,1)S(1)}, u32[]{:S(2)}) copy-start(bf16[16,2,32,512]{3,2,1,0:T(8,128)(2,1)S(1)} %multiply_convert_fusion) | copy-start | bytes 3145732
  9.6 28.2 %collective-permute-start = (bf16[16,2,32,512]{3,2,1,0:T(8,128)(2,1)S(1)}, bf16[16,2,32,512]{3,2,1,0:T(8,128)(2,1)}, u32[]{:S(2)}, u32[]{:S(2)}) collective-permute-start(bf16[16,2,32,512]{3,2,1,0:T(8,128)(2,1)S(1)} %multiply_convert_fusion), channel_id=1, source_target_pairs={{4,0},{8,4},{12,8},{5,1},{9,5},{13,9},{6,2},{10,6},{14,10},{7,3},{... | collective-permute-start | bytes 3145736 | tf_op jit(solution)/shard_map/ppermute | solution.py:19
  10.9 95.5 %collective-permute-start.1 = (bf16[16,2,32,512]{3,2,1,0:T(8,128)(2,1)S(1)}, bf16[16,2,32,512]{3,2,1,0:T(8,128)(2,1)}, u32[]{:S(2)}, u32[]{:S(2)}) collective-permute-start(bf16[16,2,32,512]{3,2,1,0:T(8,128)(2,1)S(1)} %multiply_convert_fusion), channel_id=1, source_target_pairs={{8,0},{12,4},{9,1},{13,5},{10,2},{14,6},{11,3},{15,7},{24,16},{28,... | collective-permute-start | bytes 3145736 | tf_op jit(solution)/shard_map/ppermute | solution.py:19
  12.2 94.2 %collective-permute-start.2 = (bf16[16,2,32,512]{3,2,1,0:T(8,128)(2,1)S(1)}, bf16[16,2,32,512]{3,2,1,0:T(8,128)(2,1)}, u32[]{:S(2)}, u32[]{:S(2)}) collective-permute-start(bf16[16,2,32,512]{3,2,1,0:T(8,128)(2,1)S(1)} %multiply_convert_fusion), channel_id=1, source_target_pairs={{12,0},{13,1},{14,2},{15,3},{28,16},{29,17},{30,18},{31,19}} | collective-permute-start | bytes 3145736 | tf_op jit(solution)/shard_map/ppermute | solution.py:19
  112.9 52.4 %all-to-all-start = ((bf16[16,4,2,32,512]{4,0,2,1,3:T(8,128)(2,1)}), bf16[16,4,2,32,512]{4,0,2,1,3:T(8,128)(2,1)}, u32[]{:S(2)}, u32[]{:S(2)}) async-start(bf16[16,4,2,32,512]{4,0,2,1,3:T(8,128)(2,1)} %copy.52), calls=%async_computation | async-start | bytes 8388608 | tf_op jit(solution)/shard_map/all_to_all | solution.py:72
  118.5 209.8 %reduce-scatter.2.cloned.1.call-start = ((), (), s32[]{:S(2)}) async-start(), calls=%async_computation.3 | async-start | bytes 6291456 | tf_op jit(solution)/shard_map/reduce_scatter | solution.py:74
  199.7 12.8 %copy-start = (bf16[32,4,1,16,512]{0,3,1,4,2:T(8,128)(2,1)S(1)}, bf16[32,4,1,16,512]{0,3,1,4,2:T(8,128)(2,1)}, u32[]{:S(2)}) copy-start(bf16[32,4,1,16,512]{0,3,1,4,2:T(8,128)(2,1)} %copy.64) | copy-start | bytes 6291460
  199.7 12.8 %copy-start.1 = (bf16[32,1,32,512]{2,0,3,1:T(8,128)(2,1)S(1)}, bf16[32,1,32,512]{2,0,3,1:T(8,128)(2,1)}, u32[]{:S(2)}) copy-start(bf16[32,1,32,512]{2,0,3,1:T(8,128)(2,1)} %copy.67) | copy-start | bytes 3145732
  278.9 22.9 %copy-start.3 = (f32[512,512]{1,0:T(8,128)S(1)}, f32[512,512]{1,0:T(8,128)}, u32[]{:S(2)}) copy-start(f32[512,512]{1,0:T(8,128)} %get-tuple-element.10) | copy-start | bytes 3145732
Sparse Core Ops, SparseCore 0:
  13.6 39.7 all-gather.1
  318.9 9.3 reduce-scatter.1
where the time goes:
time: 339 us; the launch traced here: 338 us
  waiting for transfers between devices  128 us (38%)
  local copies, waits for them, and re-layouts  76.3 us (23%)
  matrix products  71.7 us (21%)
  other arithmetic  39.3 us (12%)
  between operations  13.5 us (4%)
  starting transfers between devices  9.71 us (3%)
    ppermute x3, waiting for transfers between devices, shifted(): return lax.ppermute(block, axis, route)  91.9 us
    dot_general x4, matrix products, product(): return jnp.einsum(pattern, left, right, preferred_element_type=jnp.float32)  54.7 us
    unnamed x14, local copies, waits for them, and re-layouts  41.1 us
    all_to_all x1, waiting for transfers between devices, body(): lax.all_to_all(partner_local, 'win', split_axis=3, concat_axis=0, tiled=T...  26.5 us
    another operation x1, other arithmetic, cross_spectra(): return jnp.stack([real_part, imag_part], axis=3)  24.5 us
    dot_general x1, local copies, waits for them, and re-layouts, transform(): jnp.dot(flat, table, precision=lax.Precision.HIGHEST, preferred_element_t...  22.9 us
    dot_general x1, matrix products, transform(): jnp.dot(flat, table, precision=lax.Precision.HIGHEST, preferred_element_t...  16.9 us
    reduce_scatter x1, waiting for transfers between devices, body(): lax.psum_scatter(partial_value, 'lag', scatter_dimension=3, tiled=True)  9.54 us
  transfers between devices with their start and end apart: 6, of which 4 were waited for; matrix products, arithmetic and copies ran while one was open for 8% of the time, Pallas kernels for 0%

commit v1 on v0

v1 whole, which is shorter than its diff:
```python
import functools
import math

import jax
import jax.numpy as jnp
from jax import lax
from jax.experimental import pallas as pl
from jax.experimental.pallas import tpu as pltpu
from jax.sharding import PartitionSpec as P

LAGS = 512
NSAMP = 15000
FLOW = 60
LANES = 128
ROWS_AT_ONCE = 4

water_level = 0.5

MESH = pl.DeviceIdType.MESH
F32 = jnp.float32
BF16 = jnp.bfloat16


def kernel(
    sizes, spectra, mask, out, own, ybuf, xf, yf, pacc, cos_hi, cos_lo, sin_hi, sin_lo,
    outgoing, incoming, xs, xr, zs, zr, ls, lr,
):
    blocks, win, slots = sizes
    w_here, _, chans, bins = spectra.shape
    share = chans // win
    half = LAGS // 2
    c = lax.axis_index("chan")
    w = lax.axis_index("win")
    lag = lax.axis_index("lag")
    scale = (w_here * win * bins * 2) ** (-0.5)

    def lag_copy(k):
        return pltpu.make_async_remote_copy(
            outgoing.at[k], incoming.at[k], ls.at[k], lr.at[k],
            device_id={"lag": 1 - lag}, device_id_type=MESH)

    def win_send(d, n):
        peer = lax.rem(w + d, win)
        g = lax.rem(peer + n, win)
        return pltpu.make_async_remote_copy(
            own.at[w, g], own.at[w, g], xs.at[d - 1, n], xr.at[d - 1, n],
            device_id={"win": peer}, device_id_type=MESH)

    def win_arrival(d, n):
        source = lax.rem(w + win - d, win)
        g = lax.rem(w + n, win)
        return pltpu.make_async_remote_copy(
            own.at[source, g], own.at[source, g], xs.at[d - 1, n], xr.at[d - 1, n],
            device_id={"win": source}, device_id_type=MESH)

    def down(k, i):
        g = lax.rem(w + i, win)
        src = own.at[g, w] if k == 1 else ybuf.at[k - 2, i]
        return pltpu.make_async_remote_copy(
            src, ybuf.at[k - 1, i], zs.at[k - 1, i], zr.at[k - 1, i],
            device_id={"chan": c - 1}, device_id_type=MESH)

    def send_down(k, i):
        @pl.when((c >= 1) & (c + k - 1 < blocks))
        def _():
            down(k, i).start()

    barrier = pltpu.get_barrier_semaphore()
    pl.semaphore_signal(barrier, inc=1, device_id={"lag": 1 - lag}, device_id_type=MESH)
    for d in range(1, win):
        pl.semaphore_signal(barrier, inc=1, device_id={"win": lax.rem(w + d, win)}, device_id_type=MESH)

    @pl.when(c >= 1)
    def _():
        pl.semaphore_signal(barrier, inc=1, device_id={"chan": c - 1}, device_id_type=MESH)

    @pl.when(c + 1 < blocks)
    def _():
        pl.semaphore_signal(barrier, inc=1, device_id={"chan": c + 1}, device_id_type=MESH)

    def whiten(v, carry):
        re = spectra[v, 0].astype(F32)
        im = spectra[v, 1].astype(F32)
        amplitude = jnp.sqrt(re * re + im * im)
        factor = mask[:, 0:1] / jnp.maximum(amplitude, water_level)
        re = re * factor
        im = im * factor
        for g in range(win):
            rows = slice(g * share, (g + 1) * share)
            own[w, g, v] = jnp.concatenate([re[rows], im[rows]], axis=0).astype(BF16)
        return carry

    lax.fori_loop(0, w_here, whiten, 0)

    edges = (c >= 1).astype(jnp.int32) + (c + 1 < blocks).astype(jnp.int32)
    pl.semaphore_wait(barrier, win + edges)

    for d in range(1, win):
        win_send(d, 0).start()
    send_down(1, 0)
    for d in range(1, win):
        for n in range(1, win):
            win_send(d, n).start()

    def widen(group):
        def step(v, carry):
            for g in range(win):
                value = own[group, g, v].astype(F32)
                re, im = value[:share], value[share:]
                at = group * w_here + v
                for b in range(share // ROWS_AT_ONCE):
                    to = g * share // ROWS_AT_ONCE + b
                    rows = slice(b * ROWS_AT_ONCE, (b + 1) * ROWS_AT_ONCE)
                    for t, part in enumerate((re, im, re + im)):
                        xf[at, to, t * ROWS_AT_ONCE:(t + 1) * ROWS_AT_ONCE] = part[rows]
            return carry

        lax.fori_loop(0, w_here, step, 0)

    def stack_step(src, group, first):
        def convert(v, carry):
            value = src[v].astype(F32)
            re, im = value[:share], value[share:]
            yf[v, 0:share] = re
            yf[v, share:2 * share] = im
            yf[v, 2 * share:3 * share] = re - im
            return carry

        lax.fori_loop(0, w_here, convert, 0)
        tiles = bins // LANES

        def rows(n, carry):
            b = n // tiles
            a0 = b * ROWS_AT_ONCE
            col = pl.ds(pl.multiple_of(lax.rem(n, tiles) * LANES, LANES), LANES)
            total = [[None] * 3 for _ in range(ROWS_AT_ONCE)]
            for aa in range(ROWS_AT_ONCE):
                for t in range(3):
                    if first:
                        total[aa][t] = jnp.zeros((share, LANES), F32)
                    else:
                        total[aa][t] = pacc[t, pl.ds(pl.multiple_of((a0 + aa) * share, share), share), col]
            for v in range(w_here):
                y = [yf[v, t * share:(t + 1) * share, col] for t in range(3)]
                for aa in range(ROWS_AT_ONCE):
                    for t in range(3):
                        line = t * ROWS_AT_ONCE + aa
                        x = xf[group * w_here + v, b, line:line + 1, col]
                        total[aa][t] = total[aa][t] + x * y[t]
            for aa in range(ROWS_AT_ONCE):
                for t in range(3):
                    pacc[t, pl.ds(pl.multiple_of((a0 + aa) * share, share), share), col] = total[aa][t]
            return carry

        lax.fori_loop(0, (chans // ROWS_AT_ONCE) * tiles, rows, 0)

    at_once = 256 // share
    parts = chans // at_once

    def transform(k):
        def part(n, carry):
            r = pl.ds(pl.multiple_of(n * 256, 256), 256)
            p1, p2, p3 = pacc[0, r], pacc[1, r], pacc[2, r]
            re = p1 + p2
            im = p3 - p1 + p2
            re_hi = re.astype(BF16)
            re_lo = (re - re_hi.astype(F32)).astype(BF16)
            im_hi = im.astype(BF16)
            im_lo = (im - im_hi.astype(F32)).astype(BF16)
            dot = functools.partial(jnp.dot, preferred_element_type=F32)
            total = dot(re_hi, cos_hi[...]) + dot(im_hi, sin_hi[...])
            total += dot(re_lo, cos_hi[...]) + dot(im_lo, sin_hi[...])
            total += dot(re_hi, cos_lo[...]) + dot(im_hi, sin_lo[...])
            here = total[:, :half].reshape(at_once, share, half)
            there = total[:, half:].reshape(at_once, share, half)
            a = pl.ds(n * at_once, at_once)
            out[a, k] = here
            outgoing[k, a] = there
            return carry

        lax.fori_loop(0, parts, part, 0)
        lag_copy(k).start()

    def settle(k):
        lag_copy(k).wait()

        def add(n, carry):
            a = pl.ds(n * 4, 4)
            out[a, k] = (out[a, k] + incoming[k, a]) * scale
            return carry

        lax.fori_loop(0, chans // 4, add, 0)

    def phases(n, carry):
        r = pl.ds(pl.multiple_of(n * 16, 16), 16)
        bin_no = FLOW + lag * bins + n * 16 + lax.broadcasted_iota(jnp.int32, (16, LAGS), 0)
        place = lax.broadcasted_iota(jnp.int32, (16, LAGS), 1) + lag * half
        place = jnp.where(place >= LAGS, place - LAGS, place) - LAGS // 2
        product = bin_no * place
        laps = jnp.floor(product.astype(F32) * (1.0 / NSAMP)).astype(jnp.int32)
        turns = product - laps * NSAMP
        turns = jnp.where(turns < 0, turns + NSAMP, turns)
        turns = jnp.where(turns >= NSAMP, turns - NSAMP, turns)
        angle = turns.astype(F32) * (2.0 * math.pi / NSAMP)
        cos, sin = jnp.cos(angle), -jnp.sin(angle)
        hi = cos.astype(BF16)
        cos_hi[r] = hi
        cos_lo[r] = (cos - hi.astype(F32)).astype(BF16)
        hi = sin.astype(BF16)
        sin_hi[r] = hi
        sin_lo[r] = (sin - hi.astype(F32)).astype(BF16)
        return carry

    lax.fori_loop(0, bins // 16, phases, 0)

    widen(w)
    stack_step(own.at[w, w], w, True)
    for i in range(1, win):
        d = win - i
        win_arrival(d, 0).wait_recv()
        send_down(1, i)
        for n in range(1, win):
            win_arrival(d, n).wait_recv()
        group = lax.rem(w + i, win)
        widen(group)
        stack_step(own.at[group, w], group, False)
    transform(0)

    for k in range(1, slots):
        have = c + k < blocks

        @pl.when(have)
        def _(k=k):
            for i in range(win):
                down(k, i).wait_recv()
                if k + 1 < slots:
                    send_down(k + 1, i)
                stack_step(ybuf.at[k - 1, i], lax.rem(w + i, win), i == 0)
                if i == 0 and k == 1:
                    settle(0)
            if k > 1:
                settle(k - 1)
            transform(k)

        @pl.when(jnp.logical_not(have))
        def _(k=k):
            out[:, k] = jnp.zeros((chans, share, half), F32)

    for k in range(slots):
        last = (c + k < blocks) if k == slots - 1 else (c + k == blocks - 1)

        @pl.when(last)
        def _(k=k):
            settle(k)

    for k in range(1, slots):
        @pl.when((c >= 1) & (c + k - 1 < blocks))
        def _(k=k):
            for i in range(win):
                down(k, i).wait_send()

    for d in range(1, win):
        for n in range(win):
            win_send(d, n).wait_send()


def body(blocks, win, spectra, dead_mask, partners):
    w_here, _, chans, bins = spectra.shape
    slots = partners.shape[1]
    share = chans // win
    half = LAGS // 2
    mask = jnp.broadcast_to(dead_mask.astype(F32)[:, None], (chans, LANES))
    dma = pltpu.SemaphoreType.DMA
    raw = pl.pallas_call(
        functools.partial(kernel, (blocks, win, slots)),
        out_shape=jax.ShapeDtypeStruct((chans, slots, share, half), F32),
        in_specs=[pl.BlockSpec(memory_space=pltpu.VMEM)] * 2,
        out_specs=pl.BlockSpec(memory_space=pltpu.VMEM),
        scratch_shapes=[
            pltpu.VMEM((win, win, w_here, 2 * share, bins), BF16),
            pltpu.VMEM((slots - 1, win, w_here, 2 * share, bins), BF16),
            pltpu.VMEM((win * w_here, chans // ROWS_AT_ONCE, 4 * ROWS_AT_ONCE, bins), F32),
            pltpu.VMEM((w_here, 3 * share, bins), F32),
            pltpu.VMEM((3, chans * share, bins), F32),
            pltpu.VMEM((bins, LAGS), BF16),
            pltpu.VMEM((bins, LAGS), BF16),
            pltpu.VMEM((bins, LAGS), BF16),
            pltpu.VMEM((bins, LAGS), BF16),
            pltpu.VMEM((slots, chans, share, half), F32),
            pltpu.VMEM((slots, chans, share, half), F32),
            dma((win - 1, win)),
            dma((win - 1, win)),
            dma((slots - 1, win)),
            dma((slots - 1, win)),
            dma((slots,)),
            dma((slots,)),
        ],
        compiler_params=pltpu.CompilerParams(
            collective_id=0, has_side_effects=True, vmem_limit_bytes=50 * 2**20),
    )(spectra, mask)
    wanted = lax.dynamic_index_in_dim(partners, lax.axis_index("chan"), 0, keepdims=False)
    return jnp.where(wanted[None, :, None, None] >= 0, raw, 0.0)


def solution(mesh):
    placed = (P("win", None, ("groups", "chan"), "lag"), P(("groups", "chan")), P())
    return jax.shard_map(
        functools.partial(body, mesh.shape["chan"], mesh.shape["win"]),
        mesh=mesh,
        in_specs=placed,
        out_specs=P(("groups", "chan"), None, "win", "lag"),
        check_vma=False,
    )
```

time: 339 us -> 93.5 us (0.28)
  waiting for transfers between devices: 128 us -> 0 us
  Pallas kernels: 0 us -> 88.9 us
  local copies, waits for them, and re-layouts: 76.3 us -> 1.3 us
  matrix products: 71.7 us -> 0 us
  other arithmetic: 39.3 us -> 3.07 us
  between operations: 13.5 us -> 0.02 us
  starting transfers between devices: 9.71 us -> 0 us
    ppermute x3 -> x0, waiting for transfers between devices: 91.9 us -> none  [shifted(): return lax.ppermute(block, axis, route)]
    pallas_call x0 -> x1, Pallas kernels: none -> 88.9 us  [body(): pl.pallas_call(functools.partial(kernel, (blocks, win, slots)), out_shape...]
    dot_general x5 -> x0, matrix products: 71.7 us -> none  [the longest x4 54.7 us: product(): return jnp.einsum(pattern, left, right, preferred_element_type=jnp.float32)]
    unnamed x14 -> x2, local copies, waits for them, and re-layouts: 41.1 us -> 1.23 us
    all_to_all x1 -> x0, waiting for transfers between devices: 26.5 us -> none  [body(): lax.all_to_all(partner_local, 'win', split_axis=3, concat_axis=0, tiled=T...]
    another operation x2 -> x0, other arithmetic: 24.8 us -> none  [the longest x1 24.5 us: cross_spectra(): return jnp.stack([real_part, imag_part], axis=3)]
    dot_general x1 -> x0, local copies, waits for them, and re-layouts: 22.9 us -> none  [transform(): jnp.dot(flat, table, precision=lax.Precision.HIGHEST, preferred_element_t...]
    reduce_scatter x1 -> x0, waiting for transfers between devices: 9.54 us -> none  [body(): lax.psum_scatter(partial_value, 'lag', scatter_dimension=3, tiled=True)]
  transfers between devices with their start and end apart: 6 -> 0, of which waited for: 4 -> 0; matrix products, arithmetic and copies ran while one was open for 8% -> 0% of each run, Pallas kernels for 0% -> 0%
where the time goes in v1:
time: 93.5 us; the launch traced here: 93.3 us
  Pallas kernels  88.9 us (95%)
  other arithmetic  3.07 us (3%)
  local copies, waits for them, and re-layouts  1.3 us (1%)
    pallas_call x1, Pallas kernels, body(): pl.pallas_call(functools.partial(kernel, (blocks, win, slots)), out_shape...  88.9 us

profile of v1, /device:TPU:0, one launch (start us, length us, event | category | flops | bytes accessed | tf_op | source)
XLA Modules:
  0.0 93.3 jit_solution(6254333998954667962)
XLA Ops:
  0.0 0.7 convert_element_type.3
  0.7 0.1 broadcast_in_dim.20.mask
  0.7 0.0 copy-start
  0.7 1.2 %copy-done = bf16[16,2,32,512]{3,2,1,0:T(8,128)(2,1)S(1)} copy-done((bf16[16,2,32,512]{3,2,1,0:T(8,128)(2,1)S(1)}, bf16[16,2,32,512]{3,2,1,0:T(8,128)(2,1)}, u32[]{:S(2)}) %copy-start) | copy-done | bytes 1048600
  2.0 88.9 %shard_map.37 = f32[32,4,16,256]{3,2,1,0:T(8,128)S(1)} custom-call(bf16[16,2,32,512]{3,2,1,0:T(8,128)(2,1)S(1)} %copy-done, f32[32,128]{1,0:T(8,128)S(1)} %broadcast_in_dim.20.mask), custom_call_target="tpu_custom_call" | custom-call | tf_op jit(solution)/shard_map/pallas_call | solution.py:274
  90.9 0.7 compare_bitcast_fusion
  91.6 1.7 %broadcast_select_fusion = f32[32,4,16,256]{3,2,1,0:T(8,128)} fusion(f32[32,4,16,256]{3,2,1,0:T(8,128)S(1)} %shard_map.37, pred[4]{0:T(512)(128)(4,1)S(1)} %compare_bitcast_fusion), kind=kLoop, calls=%fused_computation | loop fusion | flops 524288 | bytes 4194308 | tf_op jit(solution)/shard_map/jit(_where)/select_n | solution.py:302
Async XLA Ops:
  0.7 1.2 %copy-start = (bf16[16,2,32,512]{3,2,1,0:T(8,128)(2,1)S(1)}, bf16[16,2,32,512]{3,2,1,0:T(8,128)(2,1)}, u32[]{:S(2)}) copy-start(bf16[16,2,32,512]{3,2,1,0:T(8,128)(2,1)} %spectra.1) | copy-start | bytes 3145732

commit v2 on v1

--- a/solution.py
+++ b/solution.py
@@ -22,8 +22,8 @@
 
 
 def kernel(
-    sizes, spectra, mask, out, own, ybuf, xf, yf, pacc, cos_hi, cos_lo, sin_hi, sin_lo,
-    outgoing, incoming, xs, xr, zs, zr, ls, lr,
+    sizes, spectra, mask, out, own, ybuf, below, got, xf, yf, pacc, cos_hi, cos_lo, sin_hi, sin_lo,
+    outgoing, incoming, xs, xr, zs, zr, us, ur, rs, rr, ls, lr, fs, fr,
 ):
     blocks, win, slots = sizes
     w_here, _, chans, bins = spectra.shape
@@ -59,6 +59,35 @@
         return pltpu.make_async_remote_copy(
             src, ybuf.at[k - 1, i], zs.at[k - 1, i], zr.at[k - 1, i],
             device_id={"chan": c - 1}, device_id_type=MESH)
+
+    far = slots - 1
+    gives = c + far < blocks
+    takes = (c >= 1) & (c - 1 + far < blocks)
+    at_once = 256 // share
+    parts = chans // at_once
+
+    def up(i):
+        g = lax.rem(w + i, win)
+        return pltpu.make_async_remote_copy(
+            own.at[g], below.at[g], us.at[i], ur.at[i],
+            device_id={"chan": c + 1}, device_id_type=MESH)
+
+    def far_lag(n):
+        a = pl.ds(n * at_once, at_once)
+        return pltpu.make_async_remote_copy(
+            outgoing.at[far, a], incoming.at[far, a], fs.at[n], fr.at[n],
+            device_id={"lag": 1 - lag}, device_id_type=MESH)
+
+    def far_result(n):
+        a = pl.ds(n * at_once, at_once)
+        return pltpu.make_async_remote_copy(
+            got.at[0, a], got.at[1, a], rs.at[n], rr.at[n],
+            device_id={"chan": c - 1}, device_id_type=MESH)
+
+    def send_up(i):
+        @pl.when(gives)
+        def _():
+            up(i).start()
 
     def send_down(k, i):
         @pl.when((c >= 1) & (c + k - 1 < blocks))
@@ -98,26 +127,27 @@
     for d in range(1, win):
         win_send(d, 0).start()
     send_down(1, 0)
+    send_up(0)
     for d in range(1, win):
         for n in range(1, win):
             win_send(d, n).start()
 
-    def widen(group):
+    def widen(blockref, group, which):
         def step(v, carry):
             for g in range(win):
-                value = own[group, g, v].astype(F32)
+                value = blockref[group, g, v].astype(F32)
                 re, im = value[:share], value[share:]
                 at = group * w_here + v
                 for b in range(share // ROWS_AT_ONCE):
                     to = g * share // ROWS_AT_ONCE + b
                     rows = slice(b * ROWS_AT_ONCE, (b + 1) * ROWS_AT_ONCE)
                     for t, part in enumerate((re, im, re + im)):
-                        xf[at, to, t * ROWS_AT_ONCE:(t + 1) * ROWS_AT_ONCE] = part[rows]
+                        xf[which, at, to, t * ROWS_AT_ONCE:(t + 1) * ROWS_AT_ONCE] = part[rows]
             return carry
 
         lax.fori_loop(0, w_here, step, 0)
 
-    def stack_step(src, group, first):
+    def stack_step(src, group, first, which=0):
         def convert(v, carry):
             value = src[v].astype(F32)
             re, im = value[:share], value[share:]
@@ -139,28 +169,24 @@
                     if first:
                         total[aa][t] = jnp.zeros((share, LANES), F32)
                     else:
-                        total[aa][t] = pacc[t, pl.ds(pl.multiple_of((a0 + aa) * share, share), share), col]
+                        total[aa][t] = pacc[which, t, pl.ds(pl.multiple_of((a0 + aa) * share, share), share), col]
             for v in range(w_here):
                 y = [yf[v, t * share:(t + 1) * share, col] for t in range(3)]
                 for aa in range(ROWS_AT_ONCE):
                     for t in range(3):
                         line = t * ROWS_AT_ONCE + aa
-                        x = xf[group * w_here + v, b, line:line + 1, col]
+                        x = xf[which, group * w_here + v, b, line:line + 1, col]
                         total[aa][t] = total[aa][t] + x * y[t]
             for aa in range(ROWS_AT_ONCE):
                 for t in range(3):
-                    pacc[t, pl.ds(pl.multiple_of((a0 + aa) * share, share), share), col] = total[aa][t]
+                    pacc[which, t, pl.ds(pl.multiple_of((a0 + aa) * share, share), share), col] = total[aa][t]
             return carry
 
         lax.fori_loop(0, (chans // ROWS_AT_ONCE) * tiles, rows, 0)
 
-    at_once = 256 // share
-    parts = chans // at_once
-
-    def transform(k):
-        def part(n, carry):
+    def rows_out(n, which):
             r = pl.ds(pl.multiple_of(n * 256, 256), 256)
-            p1, p2, p3 = pacc[0, r], pacc[1, r], pacc[2, r]
+            p1, p2, p3 = pacc[which, 0, r], pacc[which, 1, r], pacc[which, 2, r]
             re = p1 + p2
             im = p3 - p1 + p2
             re_hi = re.astype(BF16)
@@ -173,9 +199,12 @@
             total += dot(re_hi, cos_lo[...]) + dot(im_hi, sin_lo[...])
             here = total[:, :half].reshape(at_once, share, half)
             there = total[:, half:].reshape(at_once, share, half)
+            return here, there
+
+    def transform(k):
+        def part(n, carry):
             a = pl.ds(n * at_once, at_once)
-            out[a, k] = here
-            outgoing[k, a] = there
+            out[a, k], outgoing[k, a] = rows_out(n, 0)
             return carry
 
         lax.fori_loop(0, parts, part, 0)
@@ -213,7 +242,18 @@
 
     lax.fori_loop(0, bins // 16, phases, 0)
 
-    widen(w)
+    def far_finish():
+        for n in range(parts):
+            a = pl.ds(n * at_once, at_once)
+            got[0, a], outgoing[far, a] = rows_out(n, 1)
+            far_lag(n).start()
+        for n in range(parts):
+            a = pl.ds(n * at_once, at_once)
+            far_lag(n).wait()
+            got[0, a] = (got[0, a] + incoming[far, a]) * scale
+            far_result(n).start()
+
+    widen(own, w, 0)
     stack_step(own.at[w, w], w, True)
     for i in range(1, win):
         d = win - i
@@ -221,39 +261,65 @@
         send_down(1, i)
         for n in range(1, win):
             win_arrival(d, n).wait_recv()
+        send_up(i)
         group = lax.rem(w + i, win)
-        widen(group)
+        widen(own, group, 0)
         stack_step(own.at[group, w], group, False)
     transform(0)
 
-    for k in range(1, slots):
+    for k in range(1, far):
         have = c + k < blocks
 
         @pl.when(have)
         def _(k=k):
             for i in range(win):
+                group = lax.rem(w + i, win)
                 down(k, i).wait_recv()
-                if k + 1 < slots:
+                if k + 1 < far:
                     send_down(k + 1, i)
-                stack_step(ybuf.at[k - 1, i], lax.rem(w + i, win), i == 0)
-                if i == 0 and k == 1:
-                    settle(0)
-            if k > 1:
-                settle(k - 1)
+                else:
+                    @pl.when(takes)
+                    def _():
+                        up(i).wait_recv()
+                        widen(below, group, 1)
+                        stack_step(ybuf.at[k - 1, i], group, i == 0, 1)
+                        if i == win - 1:
+                            far_finish()
+                stack_step(ybuf.at[k - 1, i], group, i == 0)
+                if i == 0:
+                    settle(k - 1)
             transform(k)
 
         @pl.when(jnp.logical_not(have))
         def _(k=k):
             out[:, k] = jnp.zeros((chans, share, half), F32)
 
-    for k in range(slots):
-        last = (c + k < blocks) if k == slots - 1 else (c + k == blocks - 1)
+    for k in range(far):
+        last = (c + k < blocks) if k == far - 1 else (c + k == blocks - 1)
 
         @pl.when(last)
         def _(k=k):
             settle(k)
 
-    for k in range(1, slots):
+    @pl.when(gives)
+    def _():
+        for n in range(parts):
+            far_result(n).wait_recv()
+            a = pl.ds(n * at_once, at_once)
+            out[a, far] = got[1, a]
+        for i in range(win):
+            up(i).wait_send()
+
+    @pl.when(jnp.logical_not(gives))
+    def _():
+        out[:, far] = jnp.zeros((chans, share, half), F32)
+
+    @pl.when(takes)
+    def _():
+        for n in range(parts):
+            far_result(n).wait_send()
+
+    for k in range(1, far):
         @pl.when((c >= 1) & (c + k - 1 < blocks))
         def _(k=k):
             for i in range(win):
@@ -269,6 +335,7 @@
     slots = partners.shape[1]
     share = chans // win
     half = LAGS // 2
+    parts = chans * share // 256
     mask = jnp.broadcast_to(dead_mask.astype(F32)[:, None], (chans, LANES))
     dma = pltpu.SemaphoreType.DMA
     raw = pl.pallas_call(
@@ -278,10 +345,12 @@
         out_specs=pl.BlockSpec(memory_space=pltpu.VMEM),
         scratch_shapes=[
             pltpu.VMEM((win, win, w_here, 2 * share, bins), BF16),
-            pltpu.VMEM((slots - 1, win, w_here, 2 * share, bins), BF16),
-            pltpu.VMEM((win * w_here, chans // ROWS_AT_ONCE, 4 * ROWS_AT_ONCE, bins), F32),
+            pltpu.VMEM((slots - 2, win, w_here, 2 * share, bins), BF16),
+            pltpu.VMEM((win, win, w_here, 2 * share, bins), BF16),
+            pltpu.VMEM((2, chans, share, half), F32),
+            pltpu.VMEM((2, win * w_here, chans // ROWS_AT_ONCE, 4 * ROWS_AT_ONCE, bins), F32),
             pltpu.VMEM((w_here, 3 * share, bins), F32),
-            pltpu.VMEM((3, chans * share, bins), F32),
+            pltpu.VMEM((2, 3, chans * share, bins), F32),
             pltpu.VMEM((bins, LAGS), BF16),
             pltpu.VMEM((bins, LAGS), BF16),
             pltpu.VMEM((bins, LAGS), BF16),
@@ -290,13 +359,19 @@
             pltpu.VMEM((slots, chans, share, half), F32),
             dma((win - 1, win)),
             dma((win - 1, win)),
-            dma((slots - 1, win)),
-            dma((slots - 1, win)),
-            dma((slots,)),
-            dma((slots,)),
+            dma((slots - 2, win)),
+            dma((slots - 2, win)),
+            dma((win,)),
+            dma((win,)),
+            dma((parts,)),
+            dma((parts,)),
+            dma((slots - 1,)),
+            dma((slots - 1,)),
+            dma((parts,)),
+            dma((parts,)),
         ],
         compiler_params=pltpu.CompilerParams(
-            collective_id=0, has_side_effects=True, vmem_limit_bytes=50 * 2**20),
+            collective_id=0, has_side_effects=True, vmem_limit_bytes=60 * 2**20),
     )(spectra, mask)
     wanted = lax.dynamic_index_in_dim(partners, lax.axis_index("chan"), 0, keepdims=False)
     return jnp.where(wanted[None, :, None, None] >= 0, raw, 0.0)

time: 93.5 us -> 87.7 us (0.938)
  Pallas kernels: 88.9 us -> 82.1 us
  other arithmetic: 3.07 us -> 4.68 us
    pallas_call x1, Pallas kernels: 88.9 us -> 82.1 us  [body(): pl.pallas_call(functools.partial(kernel, (blocks, win, slots)), out_shape...]
    select_n x1, other arithmetic: 1.72 us -> 3.32 us  [body(): return jnp.where(wanted[None, :, None, None] >= 0, raw, 0.0)]
    unnamed x2 -> x0, local copies, waits for them, and re-layouts: 1.23 us -> none
where the time goes in v2:
time: 87.7 us; the launch traced here: 87.5 us
  Pallas kernels  82.1 us (94%)
  other arithmetic  4.68 us (5%)
    pallas_call x1, Pallas kernels, body(): pl.pallas_call(functools.partial(kernel, (blocks, win, slots)), out_shape...  82.1 us
    select_n x1, other arithmetic, body(): return jnp.where(wanted[None, :, None, None] >= 0, raw, 0.0)  3.32 us

profile of v2, /device:TPU:0, one launch (start us, length us, event | category | flops | bytes accessed | tf_op | source)
XLA Modules:
  0.0 87.5 jit_solution(18285332230379849403)
XLA Ops:
  0.0 0.7 convert_element_type.3
  0.7 0.7 broadcast_in_dim.20.mask
  1.3 82.1 %shard_map.37 = f32[32,4,16,256]{3,2,1,0:T(8,128)} custom-call(bf16[16,2,32,512]{3,2,1,0:T(8,128)(2,1)} %spectra.1, f32[32,128]{1,0:T(8,128)} %broadcast_in_dim.20.mask), custom_call_target="tpu_custom_call" | custom-call | tf_op jit(solution)/shard_map/pallas_call | solution.py:341
  83.4 0.7 compare_bitcast_fusion
  84.1 3.3 %broadcast_select_fusion = f32[32,4,16,256]{3,2,1,0:T(8,128)} fusion(f32[32,4,16,256]{3,2,1,0:T(8,128)} %shard_map.37, pred[4]{0:T(512)(128)(4,1)S(1)} %compare_bitcast_fusion), kind=kLoop, calls=%fused_computation | loop fusion | flops 524288 | bytes 4194308 | tf_op jit(solution)/shard_map/jit(_where)/select_n | solution.py:377

commit v3 on v2

--- a/solution.py
+++ b/solution.py
@@ -13,6 +13,7 @@
 FLOW = 60
 LANES = 128
 ROWS_AT_ONCE = 4
+PIECES = 4
 
 water_level = 0.5
 
@@ -53,11 +54,14 @@
             own.at[source, g], own.at[source, g], xs.at[d - 1, n], xr.at[d - 1, n],
             device_id={"win": source}, device_id_type=MESH)
 
-    def down(k, i):
+    piece = w_here // PIECES
+
+    def down(k, i, q):
         g = lax.rem(w + i, win)
         src = own.at[g, w] if k == 1 else ybuf.at[k - 2, i]
-        return pltpu.make_async_remote_copy(
-            src, ybuf.at[k - 1, i], zs.at[k - 1, i], zr.at[k - 1, i],
+        part = pl.ds(q * piece, piece)
+        return pltpu.make_async_remote_copy(
+            src.at[part], ybuf.at[k - 1, i, part], zs.at[k - 1, i, q], zr.at[k - 1, i, q],
             device_id={"chan": c - 1}, device_id_type=MESH)
 
     far = slots - 1
@@ -66,10 +70,11 @@
     at_once = 256 // share
     parts = chans // at_once
 
-    def up(i):
+    def up(i, q):
         g = lax.rem(w + i, win)
-        return pltpu.make_async_remote_copy(
-            own.at[g], below.at[g], us.at[i], ur.at[i],
+        part = pl.ds(q * piece, piece)
+        return pltpu.make_async_remote_copy(
+            own.at[g, :, part], below.at[g, :, part], us.at[i, q], ur.at[i, q],
             device_id={"chan": c + 1}, device_id_type=MESH)
 
     def far_lag(n):
@@ -87,12 +92,14 @@
     def send_up(i):
         @pl.when(gives)
         def _():
-            up(i).start()
+            for q in range(PIECES):
+                up(i, q).start()
 
     def send_down(k, i):
         @pl.when((c >= 1) & (c + k - 1 < blocks))
         def _():
-            down(k, i).start()
+            for q in range(PIECES):
+                down(k, i, q).start()
 
     barrier = pltpu.get_barrier_semaphore()
     pl.semaphore_signal(barrier, inc=1, device_id={"lag": 1 - lag}, device_id_type=MESH)
@@ -132,7 +139,7 @@
         for n in range(1, win):
             win_send(d, n).start()
 
-    def widen(blockref, group, which):
+    def widen(blockref, group, which, start, count):
         def step(v, carry):
             for g in range(win):
                 value = blockref[group, g, v].astype(F32)
@@ -145,18 +152,18 @@
                         xf[which, at, to, t * ROWS_AT_ONCE:(t + 1) * ROWS_AT_ONCE] = part[rows]
             return carry
 
-        lax.fori_loop(0, w_here, step, 0)
-
-    def stack_step(src, group, first, which=0):
+        lax.fori_loop(start, start + count, step, 0)
+
+    def stack_step(src, group, fresh, which, start, count):
         def convert(v, carry):
-            value = src[v].astype(F32)
+            value = src[start + v].astype(F32)
             re, im = value[:share], value[share:]
             yf[v, 0:share] = re
             yf[v, share:2 * share] = im
             yf[v, 2 * share:3 * share] = re - im
             return carry
 
-        lax.fori_loop(0, w_here, convert, 0)
+        lax.fori_loop(0, count, convert, 0)
         tiles = bins // LANES
 
         def rows(n, carry):
@@ -166,16 +173,18 @@
             total = [[None] * 3 for _ in range(ROWS_AT_ONCE)]
             for aa in range(ROWS_AT_ONCE):
                 for t in range(3):
-                    if first:
+                    if fresh is True:
                         total[aa][t] = jnp.zeros((share, LANES), F32)
                     else:
                         total[aa][t] = pacc[which, t, pl.ds(pl.multiple_of((a0 + aa) * share, share), share), col]
-            for v in range(w_here):
+                        if fresh is not False:
+                            total[aa][t] = jnp.where(fresh, 0.0, total[aa][t])
+            for v in range(count):
                 y = [yf[v, t * share:(t + 1) * share, col] for t in range(3)]
                 for aa in range(ROWS_AT_ONCE):
                     for t in range(3):
                         line = t * ROWS_AT_ONCE + aa
-                        x = xf[which, group * w_here + v, b, line:line + 1, col]
+                        x = xf[which, group * w_here + start + v, b, line:line + 1, col]
                         total[aa][t] = total[aa][t] + x * y[t]
             for aa in range(ROWS_AT_ONCE):
                 for t in range(3):
@@ -253,8 +262,15 @@
             got[0, a] = (got[0, a] + incoming[far, a]) * scale
             far_result(n).start()
 
-    widen(own, w, 0)
-    stack_step(own.at[w, w], w, True)
+    def take(k, i):
+        @pl.when(c + k < blocks)
+        def _():
+            for q in range(PIECES):
+                down(k, i, q).wait_recv()
+        send_down(k + 1, i)
+
+    widen(own, w, 0, 0, w_here)
+    stack_step(own.at[w, w], w, True, 0, 0, w_here)
     for i in range(1, win):
         d = win - i
         win_arrival(d, 0).wait_recv()
@@ -262,10 +278,19 @@
         for n in range(1, win):
             win_arrival(d, n).wait_recv()
         send_up(i)
+        take(1, i - 1)
         group = lax.rem(w + i, win)
-        widen(own, group, 0)
-        stack_step(own.at[group, w], group, False)
+        widen(own, group, 0, 0, w_here)
+        stack_step(own.at[group, w], group, False, 0, 0, w_here)
+    take(1, win - 1)
     transform(0)
+
+    def far_step(k, i, q):
+        group = lax.rem(w + i, win)
+        start = q * piece
+        up(i, q).wait_recv()
+        widen(below, group, 1, start, piece)
+        stack_step(ybuf.at[k - 1, i], group, (q == 0) if i == 0 else False, 1, start, piece)
 
     for k in range(1, far):
         have = c + k < blocks
@@ -274,18 +299,21 @@
         def _(k=k):
             for i in range(win):
                 group = lax.rem(w + i, win)
-                down(k, i).wait_recv()
-                if k + 1 < far:
-                    send_down(k + 1, i)
-                else:
-                    @pl.when(takes)
-                    def _():
-                        up(i).wait_recv()
-                        widen(below, group, 1)
-                        stack_step(ybuf.at[k - 1, i], group, i == 0, 1)
-                        if i == win - 1:
-                            far_finish()
-                stack_step(ybuf.at[k - 1, i], group, i == 0)
+                if k + 1 == far:
+                    def arrive(q, carry):
+                        down(k, i, q).wait_recv()
+
+                        @pl.when(takes)
+                        def _():
+                            far_step(k, i, q)
+                        return carry
+
+                    lax.fori_loop(0, PIECES, arrive, 0)
+                    if i == win - 1:
+                        pl.when(takes)(far_finish)
+                elif k > 1:
+                    take(k, i)
+                stack_step(ybuf.at[k - 1, i], group, i == 0, 0, 0, w_here)
                 if i == 0:
                     settle(k - 1)
             transform(k)
@@ -308,7 +336,8 @@
             a = pl.ds(n * at_once, at_once)
             out[a, far] = got[1, a]
         for i in range(win):
-            up(i).wait_send()
+            for q in range(PIECES):
+                up(i, q).wait_send()
 
     @pl.when(jnp.logical_not(gives))
     def _():
@@ -323,7 +352,8 @@
         @pl.when((c >= 1) & (c + k - 1 < blocks))
         def _(k=k):
             for i in range(win):
-                down(k, i).wait_send()
+                for q in range(PIECES):
+                    down(k, i, q).wait_send()
 
     for d in range(1, win):
         for n in range(win):
@@ -359,10 +389,10 @@
             pltpu.VMEM((slots, chans, share, half), F32),
             dma((win - 1, win)),
             dma((win - 1, win)),
-            dma((slots - 2, win)),
-            dma((slots - 2, win)),
-            dma((win,)),
-            dma((win,)),
+            dma((slots - 2, win, PIECES)),
+            dma((slots - 2, win, PIECES)),
+            dma((win, PIECES)),
+            dma((win, PIECES)),
             dma((parts,)),
             dma((parts,)),
             dma((slots - 1,)),
@@ -371,7 +401,7 @@
             dma((parts,)),
         ],
         compiler_params=pltpu.CompilerParams(
-            collective_id=0, has_side_effects=True, vmem_limit_bytes=60 * 2**20),
+            collective_id=0, has_side_effects=True, vmem_limit_bytes=(44 if win == 2 else 60) * 2**20),
     )(spectra, mask)
     wanted = lax.dynamic_index_in_dim(partners, lax.axis_index("chan"), 0, keepdims=False)
     return jnp.where(wanted[None, :, None, None] >= 0, raw, 0.0)

time: 87.7 us -> 85.1 us (0.970)
  other arithmetic: 4.68 us -> 3.07 us
  Pallas kernels: 82.1 us -> 80.5 us
    select_n x1, other arithmetic: 3.32 us -> 1.72 us  [body(): return jnp.where(wanted[None, :, None, None] >= 0, raw, 0.0)]
    pallas_call x1, Pallas kernels: 82.1 us -> 80.5 us  [body(): pl.pallas_call(functools.partial(kernel, (blocks, win, slots)), out_shape...]
    unnamed x0 -> x2, local copies, waits for them, and re-layouts: none -> 1.23 us
where the time goes in v3:
time: 85.1 us; the launch traced here: 84.9 us
  Pallas kernels  80.5 us (95%)
  other arithmetic  3.07 us (4%)
  local copies, waits for them, and re-layouts  1.3 us (2%)
    pallas_call x1, Pallas kernels, body(): pl.pallas_call(functools.partial(kernel, (blocks, win, slots)), out_shape...  80.5 us
    select_n x1, other arithmetic, body(): return jnp.where(wanted[None, :, None, None] >= 0, raw, 0.0)  1.72 us

profile of v3, /device:TPU:0, one launch (start us, length us, event | category | flops | bytes accessed | tf_op | source)
XLA Modules:
  0.0 84.9 jit_solution(11664190562393787741)
XLA Ops:
  0.0 0.7 convert_element_type.3
  0.7 0.1 broadcast_in_dim.20.mask
  0.7 0.0 copy-start
  0.7 1.2 %copy-done = bf16[16,2,32,512]{3,2,1,0:T(8,128)(2,1)S(1)} copy-done((bf16[16,2,32,512]{3,2,1,0:T(8,128)(2,1)S(1)}, bf16[16,2,32,512]{3,2,1,0:T(8,128)(2,1)}, u32[]{:S(2)}) %copy-start) | copy-done | bytes 1048600
  2.0 80.5 %shard_map.37 = f32[32,4,16,256]{3,2,1,0:T(8,128)S(1)} custom-call(bf16[16,2,32,512]{3,2,1,0:T(8,128)(2,1)S(1)} %copy-done, f32[32,128]{1,0:T(8,128)S(1)} %broadcast_in_dim.20.mask), custom_call_target="tpu_custom_call" | custom-call | tf_op jit(solution)/shard_map/pallas_call | solution.py:371
  82.5 0.7 compare_bitcast_fusion
  83.2 1.7 %broadcast_select_fusion = f32[32,4,16,256]{3,2,1,0:T(8,128)} fusion(f32[32,4,16,256]{3,2,1,0:T(8,128)S(1)} %shard_map.37, pred[4]{0:T(512)(128)(4,1)S(1)} %compare_bitcast_fusion), kind=kLoop, calls=%fused_computation | loop fusion | flops 524288 | bytes 4194308 | tf_op jit(solution)/shard_map/jit(_where)/select_n | solution.py:407
Async XLA Ops:
  0.7 1.2 %copy-start = (bf16[16,2,32,512]{3,2,1,0:T(8,128)(2,1)S(1)}, bf16[16,2,32,512]{3,2,1,0:T(8,128)(2,1)}, u32[]{:S(2)}) copy-start(bf16[16,2,32,512]{3,2,1,0:T(8,128)(2,1)} %spectra.1) | copy-start | bytes 3145732

commit v4 on v3

--- a/solution.py
+++ b/solution.py
@@ -184,7 +184,7 @@
                 for aa in range(ROWS_AT_ONCE):
                     for t in range(3):
                         line = t * ROWS_AT_ONCE + aa
-                        x = xf[which, group * w_here + start + v, b, line:line + 1, col]
+                        x = xf[which % 2, group * w_here + start + v, b, line:line + 1, col]
                         total[aa][t] = total[aa][t] + x * y[t]
             for aa in range(ROWS_AT_ONCE):
                 for t in range(3):
@@ -210,10 +210,10 @@
             there = total[:, half:].reshape(at_once, share, half)
             return here, there
 
-    def transform(k):
+    def transform(k, which=0):
         def part(n, carry):
             a = pl.ds(n * at_once, at_once)
-            out[a, k], outgoing[k, a] = rows_out(n, 0)
+            out[a, k], outgoing[k, a] = rows_out(n, which)
             return carry
 
         lax.fori_loop(0, parts, part, 0)
@@ -272,17 +272,22 @@
     widen(own, w, 0, 0, w_here)
     stack_step(own.at[w, w], w, True, 0, 0, w_here)
     for i in range(1, win):
-        d = win - i
-        win_arrival(d, 0).wait_recv()
+        win_arrival(win - i, 0).wait_recv()
         send_down(1, i)
+    take(1, 0)
+
+    @pl.when(c + 1 < blocks)
+    def _():
+        stack_step(ybuf.at[0, 0], w, True, 2, 0, w_here)
+
+    for i in range(1, win):
         for n in range(1, win):
-            win_arrival(d, n).wait_recv()
+            win_arrival(win - i, n).wait_recv()
         send_up(i)
-        take(1, i - 1)
         group = lax.rem(w + i, win)
         widen(own, group, 0, 0, w_here)
         stack_step(own.at[group, w], group, False, 0, 0, w_here)
-    take(1, win - 1)
+        take(1, i)
     transform(0)
 
     def far_step(k, i, q):
@@ -313,10 +318,13 @@
                         pl.when(takes)(far_finish)
                 elif k > 1:
                     take(k, i)
-                stack_step(ybuf.at[k - 1, i], group, i == 0, 0, 0, w_here)
-                if i == 0:
+                if k > 1 or i > 0:
+                    stack_step(ybuf.at[k - 1, i], group, i == 0, 2 if k == 1 else 0, 0, w_here)
+                if i == 0 and k > 1:
                     settle(k - 1)
-            transform(k)
+            transform(k, 2 if k == 1 else 0)
+            if k == 1:
+                settle(0)
 
         @pl.when(jnp.logical_not(have))
         def _(k=k):
@@ -380,7 +388,7 @@
             pltpu.VMEM((2, chans, share, half), F32),
             pltpu.VMEM((2, win * w_here, chans // ROWS_AT_ONCE, 4 * ROWS_AT_ONCE, bins), F32),
             pltpu.VMEM((w_here, 3 * share, bins), F32),
-            pltpu.VMEM((2, 3, chans * share, bins), F32),
+            pltpu.VMEM((3, 3, chans * share, bins), F32),
             pltpu.VMEM((bins, LAGS), BF16),
             pltpu.VMEM((bins, LAGS), BF16),
             pltpu.VMEM((bins, LAGS), BF16),
@@ -401,7 +409,7 @@
             dma((parts,)),
         ],
         compiler_params=pltpu.CompilerParams(
-            collective_id=0, has_side_effects=True, vmem_limit_bytes=(44 if win == 2 else 60) * 2**20),
+            collective_id=0, has_side_effects=True, vmem_limit_bytes=(47 if win == 2 else 60) * 2**20),
     )(spectra, mask)
     wanted = lax.dynamic_index_in_dim(partners, lax.axis_index("chan"), 0, keepdims=False)
     return jnp.where(wanted[None, :, None, None] >= 0, raw, 0.0)

time: 85.1 us -> 81.3 us (0.955)
  Pallas kernels: 80.5 us -> 76.7 us
    pallas_call x1, Pallas kernels: 80.5 us -> 76.7 us  [body(): pl.pallas_call(functools.partial(kernel, (blocks, win, slots)), out_shape...]
where the time goes in v4:
time: 81.3 us; the launch traced here: 81.1 us
  Pallas kernels  76.7 us (94%)
  other arithmetic  3.07 us (4%)
  local copies, waits for them, and re-layouts  1.3 us (2%)
    pallas_call x1, Pallas kernels, body(): pl.pallas_call(functools.partial(kernel, (blocks, win, slots)), out_shape...  76.7 us
    select_n x1, other arithmetic, body(): return jnp.where(wanted[None, :, None, None] >= 0, raw, 0.0)  1.72 us

profile of v4, /device:TPU:0, one launch (start us, length us, event | category | flops | bytes accessed | tf_op | source)
XLA Modules:
  0.0 81.1 jit_solution(15274619879984948765)
XLA Ops:
  0.0 0.7 convert_element_type.3
  0.7 0.1 broadcast_in_dim.20.mask
  0.7 0.0 copy-start
  0.7 1.2 %copy-done = bf16[16,2,32,512]{3,2,1,0:T(8,128)(2,1)S(1)} copy-done((bf16[16,2,32,512]{3,2,1,0:T(8,128)(2,1)S(1)}, bf16[16,2,32,512]{3,2,1,0:T(8,128)(2,1)}, u32[]{:S(2)}) %copy-start) | copy-done | bytes 1048600
  2.0 76.7 %shard_map.37 = f32[32,4,16,256]{3,2,1,0:T(8,128)S(1)} custom-call(bf16[16,2,32,512]{3,2,1,0:T(8,128)(2,1)S(1)} %copy-done, f32[32,128]{1,0:T(8,128)S(1)} %broadcast_in_dim.20.mask), custom_call_target="tpu_custom_call" | custom-call | tf_op jit(solution)/shard_map/pallas_call | solution.py:379
  78.7 0.7 compare_bitcast_fusion
  79.4 1.7 %broadcast_select_fusion = f32[32,4,16,256]{3,2,1,0:T(8,128)} fusion(f32[32,4,16,256]{3,2,1,0:T(8,128)S(1)} %shard_map.37, pred[4]{0:T(512)(128)(4,1)S(1)} %compare_bitcast_fusion), kind=kLoop, calls=%fused_computation | loop fusion | flops 524288 | bytes 4194308 | tf_op jit(solution)/shard_map/jit(_where)/select_n | solution.py:415
Async XLA Ops:
  0.7 1.2 %copy-start = (bf16[16,2,32,512]{3,2,1,0:T(8,128)(2,1)S(1)}, bf16[16,2,32,512]{3,2,1,0:T(8,128)(2,1)}, u32[]{:S(2)}) copy-start(bf16[16,2,32,512]{3,2,1,0:T(8,128)(2,1)} %spectra.1) | copy-start | bytes 3145732
